TPU v7x, 512 devices: a whole 4x8x8 slice. The times are simulated.
512 devices in a mesh: dp: 16 (over y, core), ctx: 32 (over x, z).
Axes of the slice: x: 4, y: 8, z: 8, core: 2. Of those that a mesh axis runs over, the one named last changes fastest.
Arguments:
- query_proj: bfloat16 [4096, 8192], P('ctx', 'dp'), may hold values from -6 to 6
- key_proj: bfloat16 [4096, 8192], P('ctx', 'dp'), may hold values from -6 to 6
- value_proj: bfloat16 [4096, 8192], P('ctx', 'dp'), may hold values from -6 to 6
- short_taps: bfloat16 [3, 7, 8192], P(None, None, 'dp'), may hold values from -2 to 2
- medium_taps: bfloat16 [512, 128], P('dp'), may hold values from -0.5 to 0.5
- out_grad: bfloat16 [4096, 8192], P('ctx', 'dp'), may hold values from -0.09375 to 0.09375
Outputs:
- short_grad: float32 [3, 7, 8192], P(None, None, 'dp')
- medium_grad: float32 [512, 128], P('dp')
All inputs are finite; a program needn't handle non-finite values.
Results may differ from a plain program's by a relative error of at most 0.0003.
Values may be sent and summed in bfloat16 or wider, within the bound.
A program may use at most 64 MiB of HBM per device.

v0:
```python
import jax
import jax.numpy as jnp
from jax import lax
from jax.sharding import PartitionSpec as P

highest = lax.Precision.HIGHEST


def passed_along(block, axis, distance):
    devices = range(lax.axis_size(axis))
    route = [(i - distance, i) for i in devices if i - distance in devices]
    return lax.ppermute(block, axis, route)


def featurize(extended, weights):
    tap_count = weights.shape[0]
    out_rows = extended.shape[0] - tap_count + 1
    summed = jnp.zeros((out_rows, extended.shape[1]), jnp.float32)
    for offset in range(tap_count):
        start_row = tap_count - 1 - offset
        summed = summed + weights[offset] * lax.slice_in_dim(
            extended, start_row, start_row + out_rows, axis=0
        )
    return summed


def tap_grads(grad_feat, extended, tap_count):
    own_rows = grad_feat.shape[0]
    rim_rows = tap_count - 1
    return jnp.stack(
        [
            jnp.sum(
                grad_feat
                * lax.slice_in_dim(
                    extended, rim_rows - offset, rim_rows - offset + own_rows, axis=0
                ),
                axis=0,
            )
            for offset in range(tap_count)
        ]
    )


def toeplitz(filter_block, out_rows, in_rows):
    tap_count = filter_block.shape[1]
    row_ids = lax.broadcasted_iota(jnp.int32, (out_rows, in_rows), 0)
    col_ids = lax.broadcasted_iota(jnp.int32, (out_rows, in_rows), 1)
    lag_ids = row_ids - col_ids + (tap_count - 1)
    inside = (lag_ids >= 0) & (lag_ids < tap_count)
    picked = jnp.take(filter_block, jnp.clip(lag_ids, 0, tap_count - 1), axis=1)
    return jnp.where(inside[None], picked, 0.0)


def medium_apply(field_ext, matrix, group_count, reach):
    own_rows = field_ext.shape[0] - reach
    tile_rows = matrix.shape[1]
    tile_count = own_rows // tile_rows
    window_rows = tile_rows + reach
    channels = field_ext.shape[1]
    group_size = channels // group_count

    def apply_tile(tile_index):
        field_tile = field_ext
        field_tile = field_tile.reshape(window_rows, group_count, group_size)
        return jnp.einsum(
            "gts,sgc->tgc",
            matrix,
            field_tile,
            precision=highest,
            preferred_element_type=jnp.float32,
        )

    tile_outs = lax.map(apply_tile, jnp.arange(tile_count, dtype=jnp.int32))
    return tile_outs.reshape(own_rows, channels)


def filter_gradient(grad_rows, field_ext, group_count, tap_count):
    reach = tap_count - 1
    own_rows = grad_rows.shape[0]
    tile_rows = min(128, own_rows)
    tile_count = own_rows // tile_rows
    window_rows = tile_rows + reach
    channels = grad_rows.shape[1]
    group_size = channels // group_count

    def one_tile(tile_index):
        grad_tile = grad_rows
        grad_tile = grad_tile.reshape(tile_rows, group_count, group_size)
        field_tile = field_ext
        field_tile = field_tile.reshape(window_rows, group_count, group_size)
        outer_prod = jnp.einsum(
            "tgc,sgc->gts",
            grad_tile,
            field_tile,
            precision=highest,
            preferred_element_type=jnp.float32,
        )
        flattened = outer_prod.reshape(group_count, tile_rows * window_rows)
        flattened = jnp.pad(flattened, ((0, 0), (0, tile_rows)))
        skewed = flattened.reshape(group_count, tile_rows, window_rows + 1)[:, :, :tap_count]
        return jnp.sum(skewed, axis=1)[:, ::-1]

    tile_sums = lax.map(one_tile, jnp.arange(tile_count, dtype=jnp.int32))
    return jnp.sum(tile_sums, axis=0)


def local(query_proj, key_proj, value_proj, short_taps, medium_taps, out_grad):
    conv_taps = short_taps.astype(jnp.float32)
    filter_taps = medium_taps.astype(jnp.float32)
    tap_count = filter_taps.shape[1]
    reach = tap_count - 1
    short_len = conv_taps.shape[1]
    rim_rows = short_len - 1
    group_count = filter_taps.shape[0]
    own_rows = query_proj.shape[0]
    tile_rows = min(128, own_rows)
    matrix = toeplitz(filter_taps, tile_rows, tile_rows + reach)
    rim_parts = passed_along(
        (query_proj[-rim_rows:], key_proj[-rim_rows:], value_proj[-rim_rows:]), "ctx", 1
    )
    query_ext = jnp.concatenate([rim_parts[0], query_proj]).astype(jnp.float32)
    key_ext = jnp.concatenate([rim_parts[1], key_proj]).astype(jnp.float32)
    value_ext = jnp.concatenate([rim_parts[2], value_proj]).astype(jnp.float32)
    key_feat = featurize(key_ext, conv_taps[1])
    value_feat = featurize(value_ext, conv_taps[2])
    mixed = key_feat * value_feat
    mixed_prev = passed_along(mixed[own_rows - reach :], "ctx", 1)
    mixed_ext = jnp.concatenate([mixed_prev, mixed])
    query_feat = featurize(query_ext, conv_taps[0])
    mixed_conv = medium_apply(mixed_ext, matrix, group_count, reach)
    grad_output = out_grad.astype(jnp.float32)
    grad_query_feat = grad_output * mixed_conv
    grad_conv = grad_output * query_feat
    medium_grad = filter_gradient(grad_conv, mixed_ext, group_count, tap_count)
    grad_next = passed_along(grad_conv[:reach], "ctx", -1)
    grad_ext = jnp.concatenate([grad_conv, grad_next])
    grad_mixed = medium_apply(grad_ext[::-1], matrix, group_count, reach)[::-1]
    grad_key_feat = grad_mixed * value_feat
    grad_value_feat = grad_mixed * key_feat
    short_grad = jnp.stack(
        [
            tap_grads(grad_query_feat, query_ext, short_len),
            tap_grads(grad_key_feat, key_ext, short_len),
            tap_grads(grad_value_feat, value_ext, short_len),
        ]
    )
    short_grad, medium_grad = lax.psum((short_grad, medium_grad), "ctx")
    return (short_grad, medium_grad)


def solution(mesh):
    return jax.shard_map(
        local,
        mesh=mesh,
        in_specs=(
            P("ctx", "dp"),
            P("ctx", "dp"),
            P("ctx", "dp"),
            P(None, None, "dp"),
            P("dp", None),
            P("ctx", "dp"),
        ),
        out_specs=(P(None, None, "dp"), P("dp", None)),
        check_vma=False,
    )
```

profile of v0, /device:TPU:56, one launch (start us, length us, event | category | flops | bytes accessed | tf_op | source)
XLA Modules:
  0.0 284.9 jit_solution(15652804071356602535)
XLA Ops:
  0.6 0.0 copy-start
  0.6 0.0 copy-start.2
  0.7 0.7 slice.212
  1.4 4.3 %collective-permute-start = (bf16[6,512]{1,0:T(8,128)(2,1)S(1)}, bf16[6,512]{1,0:T(8,128)(2,1)S(1)}, u32[]{:S(2)}, u32[]{:S(2)}) collective-permute-start(bf16[6,512]{1,0:T(8,128)(2,1)S(1)} %slice.212), channel_id=1, source_target_pairs={{0,1},{1,2},{2,3},{3,4},{4,5},{5,6},{6,7},{7,8},{8,9},{9,10},{10,1... | collective-permute-start | bytes 18440 | tf_op jit(solution)/shard_map/ppermute | solution.py:12
  5.7 0.7 slice.227
  6.4 4.3 %collective-permute-start.1 = (bf16[6,512]{1,0:T(8,128)(2,1)S(1)}, bf16[6,512]{1,0:T(8,128)(2,1)S(1)}, u32[]{:S(2)}, u32[]{:S(2)}) collective-permute-start(bf16[6,512]{1,0:T(8,128)(2,1)S(1)} %slice.227), channel_id=1, source_target_pairs={{0,1},{1,2},{2,3},{3,4},{4,5},{5,6},{6,7},{7,8},{8,9},{9,10},{10,1... | collective-permute-start | bytes 18440 | tf_op jit(solution)/shard_map/ppermute | solution.py:12
  10.6 0.7 slice.242
  11.3 0.2 copy.26
  11.5 4.3 %collective-permute-start.3 = (bf16[6,512]{0,1:T(8,128)(2,1)S(1)}, bf16[6,512]{0,1:T(8,128)(2,1)S(1)}, u32[]{:S(2)}, u32[]{:S(2)}) collective-permute-start(bf16[6,512]{0,1:T(8,128)(2,1)S(1)} %copy.26), channel_id=1, source_target_pairs={{0,1},{1,2},{2,3},{3,4},{4,5},{5,6},{6,7},{7,8},{8,9},{9,10},{10,1... | collective-permute-start | bytes 18440 | tf_op jit(solution)/shard_map/ppermute | solution.py:12
  15.8 1.2 fusion.24
  17.0 0.7 fusion.25
  17.8 0.3 reshape.130
  18.1 0.0 collective-permute-done
  18.1 0.9 maximum_convert_fusion.1
  19.1 0.0 collective-permute-done.1
  19.1 0.9 maximum_convert_fusion.2
  20.0 0.4 fusion.22
  20.5 5.5 %collective-permute-start.2 = (f32[127,512]{1,0:T(8,128)S(1)}, f32[127,512]{1,0:T(8,128)S(1)}, u32[]{:S(2)}, u32[]{:S(2)}) collective-permute-start(f32[127,512]{1,0:T(8,128)S(1)} %slice.289), channel_id=1, source_target_pairs={{0,1},{1,2},{2,3},{3,4},{4,5},{5,6},{6,7},{7,8},{8,9},{9,10},{10,1... | collective-permute-start | bytes 780296 | tf_op jit(solution)/shard_map/ppermute | solution.py:12
  26.0 0.1 fusion.16
  26.1 0.0 copy-done
  26.1 0.1 copy.27
  26.3 0.0 copy-done.2
  26.3 0.1 copy.24
  26.4 60.6 %gather_fusion = f32[32640,32]{1,0:T(8,128)} fusion(f32[32,128]{0,1:T(8,128)S(1)} %copy.24, s32[32768]{0:T(1024)S(1)} %pad_clamp_fusion), kind=kCustom, calls=%fused_computation | custom fusion | bytes 8486400 | tf_op jit(solution)/shard_map/jit(_take)/gather | solution.py:50
  86.9 11.6 %copy.25 = f32[32640,32]{0,1:T(8,128)} copy(f32[32640,32]{1,0:T(8,128)} %gather_fusion) | data formatting | bytes 8355840 | tf_op jit(solution)/shard_map/jit(_take)/gather | solution.py:50
  98.5 0.0 copy-start.1
  98.5 9.4 %reshape.133 = f32[128,255,32]{1,0,2:T(8,128)} reshape(f32[32640,32]{0,1:T(8,128)} %copy.25) | data formatting | bytes 8355840 | tf_op jit(solution)/shard_map/jit(_take)/gather | solution.py:50
  107.9 0.0 copy-done.1
  107.9 0.1 copy.22
  108.0 0.0 collective-permute-done.3
  108.0 0.1 maximum_convert_fusion
  108.2 0.0 collective-permute-done.2
  108.3 0.2 copy.23
  108.5 5.5 %fusion.2 = f32[32,16,128]{2,1,0:T(8,128)S(1)} fusion(f32[255,32,16]{0,2,1:T(8,128)S(1)} %bitcast.74, f32[128,255,32]{1,0,2:T(8,128)} %reshape.133, pred[128,255]{1,0:T(8,128)(4,1)S(1)} %get-tuple-element.90, pred[128,255]{1,0:T(8,128)(4,1)S(1)} %get-tuple-element.89), kind=kOutput, calls=%fused_computation.3 | convolution fusion | flops 202629120 | bytes 5027584 | tf_op jit(solution)/shard_map/while/body/eval_jaxpr/gts,sgc->tgc/dot_general | solution.py:65
  113.9 1.0 convert_multiply_fusion.1
  114.9 5.1 %fusion.26 = f32[32,128,255]{2,1,0:T(8,128)} fusion(f32[128,32,16]{0,2,1:T(8,128)S(1)} %bitcast.76, f32[255,32,16]{0,2,1:T(8,128)S(1)} %bitcast.75), kind=kOutput, calls=%fused_computation.64 | convolution fusion | flops 200540160 | bytes 4962304 | tf_op jit(solution)/shard_map/while/body/eval_jaxpr/tgc,sgc->gts/dot_general | solution.py:91
  120.0 5.2 %reshape.126 = f32[32,32640]{1,0:T(8,128)} reshape(f32[32,128,255]{2,1,0:T(8,128)} %fusion.26) | data formatting | bytes 8355840 | tf_op jit(solution)/shard_map/while/body/eval_jaxpr/reshape | solution.py:98
  125.2 2.5 pad.5
  127.6 1.3 copy.29
  128.9 1.5 collective-permute-start.4
  130.4 0.2 slice_reduce_fusion
  130.6 0.1 rev.12
  130.6 1.0 multiply_reduce_fusion.14
  131.7 6.1 %collective-permute-done.4 = f32[127,512]{0,1:T(8,128)S(1)} collective-permute-done((f32[127,512]{0,1:T(8,128)S(1)}, f32[127,512]{0,1:T(8,128)S(1)}, u32[]{:S(2)}, u32[]{:S(2)}) %collective-permute-start.4) | collective-permute-done | bytes 260128 | tf_op jit(solution)/shard_map/ppermute | solution.py:12
  137.8 0.7 reverse
  138.5 0.2 slice.349
  138.7 5.5 %fusion = f32[32,16,128]{2,1,0:T(8,128)S(1)} fusion(f32[255,32,16]{0,2,1:T(8,128)S(1)} %bitcast.78, f32[128,255,32]{1,0,2:T(8,128)} %reshape.133, pred[128,255]{1,0:T(8,128)(4,1)S(1)} %get-tuple-element.90, pred[128,255]{1,0:T(8,128)(4,1)S(1)} %get-tuple-element.89), kind=kOutput, calls=%fused_computation.1 | convolution fusion | flops 202629120 | bytes 5027584 | tf_op jit(solution)/shard_map/while/body/eval_jaxpr/gts,sgc->tgc/dot_general | solution.py:65
  144.2 0.1 copy.28
  144.3 0.1 rev.11
  144.5 0.1 fusion.23
  144.5 0.3 multiply_reduce_fusion.7
  144.8 0.3 multiply_reduce_fusion
  145.2 139.7 %all-reduce.1 = (f32[3,7,512]{2,1,0:T(8,128)}, f32[32,128]{1,0:T(8,128)}) all-reduce(f32[3,7,512]{2,1,0:T(8,128)S(1)} %pad_maximum_fusion.2, f32[32,128]{1,0:T(8,128)S(1)} %rev.12), channel_id=1, replica_groups=mesh['dp'=16,'ctx'=32] {'ctx'}, use_global_device_ids=true, to_apply=%region_21.22 | all-reduce | flops 14848 | bytes 118784 | tf_op jit(solution)/shard_map/psum | solution.py:147
  (9 shorter events, 0.3 us)
Async XLA Ops:
  0.6 25.5 %copy-start = (bf16[128,512]{1,0:T(8,128)(2,1)S(1)}, bf16[128,512]{1,0:T(8,128)(2,1)}, u32[]{:S(2)}) copy-start(bf16[128,512]{1,0:T(8,128)(2,1)} %param.6) | copy-start | bytes 393220
  0.6 25.6 %copy-start.2 = (bf16[32,128]{1,0:T(8,128)(2,1)S(1)}, bf16[32,128]{1,0:T(8,128)(2,1)}, u32[]{:S(2)}) copy-start(bf16[32,128]{1,0:T(8,128)(2,1)} %param.10) | copy-start | bytes 24580
  1.4 16.7 %collective-permute-start = (bf16[6,512]{1,0:T(8,128)(2,1)S(1)}, bf16[6,512]{1,0:T(8,128)(2,1)S(1)}, u32[]{:S(2)}, u32[]{:S(2)}) collective-permute-start(bf16[6,512]{1,0:T(8,128)(2,1)S(1)} %slice.212), channel_id=1, source_target_pairs={{0,1},{1,2},{2,3},{3,4},{4,5},{5,6},{6,7},{7,8},{8,9},{9,10},{10,1... | collective-permute-start | bytes 18440 | tf_op jit(solution)/shard_map/ppermute | solution.py:12
  6.4 12.7 %collective-permute-start.1 = (bf16[6,512]{1,0:T(8,128)(2,1)S(1)}, bf16[6,512]{1,0:T(8,128)(2,1)S(1)}, u32[]{:S(2)}, u32[]{:S(2)}) collective-permute-start(bf16[6,512]{1,0:T(8,128)(2,1)S(1)} %slice.227), channel_id=1, source_target_pairs={{0,1},{1,2},{2,3},{3,4},{4,5},{5,6},{6,7},{7,8},{8,9},{9,10},{10,1... | collective-permute-start | bytes 18440 | tf_op jit(solution)/shard_map/ppermute | solution.py:12
  11.5 96.5 %collective-permute-start.3 = (bf16[6,512]{0,1:T(8,128)(2,1)S(1)}, bf16[6,512]{0,1:T(8,128)(2,1)S(1)}, u32[]{:S(2)}, u32[]{:S(2)}) collective-permute-start(bf16[6,512]{0,1:T(8,128)(2,1)S(1)} %copy.26), channel_id=1, source_target_pairs={{0,1},{1,2},{2,3},{3,4},{4,5},{5,6},{6,7},{7,8},{8,9},{9,10},{10,1... | collective-permute-start | bytes 18440 | tf_op jit(solution)/shard_map/ppermute | solution.py:12
  20.5 87.7 %collective-permute-start.2 = (f32[127,512]{1,0:T(8,128)S(1)}, f32[127,512]{1,0:T(8,128)S(1)}, u32[]{:S(2)}, u32[]{:S(2)}) collective-permute-start(f32[127,512]{1,0:T(8,128)S(1)} %slice.289), channel_id=1, source_target_pairs={{0,1},{1,2},{2,3},{3,4},{4,5},{5,6},{6,7},{7,8},{8,9},{9,10},{10,1... | collective-permute-start | bytes 780296 | tf_op jit(solution)/shard_map/ppermute | solution.py:12
  98.5 9.4 %copy-start.1 = (bf16[128,512]{1,0:T(8,128)(2,1)S(1)}, bf16[128,512]{1,0:T(8,128)(2,1)}, u32[]{:S(2)}) copy-start(bf16[128,512]{1,0:T(8,128)(2,1)} %param.11) | copy-start | bytes 393220
  128.9 8.8 %collective-permute-start.4 = (f32[127,512]{0,1:T(8,128)S(1)}, f32[127,512]{0,1:T(8,128)S(1)}, u32[]{:S(2)}, u32[]{:S(2)}) collective-permute-start(f32[127,512]{0,1:T(8,128)S(1)} %bitcast.77), channel_id=1, source_target_pairs={{1,0},{2,1},{3,2},{4,3},{5,4},{6,5},{7,6},{8,7},{9,8},{10,9},{11,1... | collective-permute-start | bytes 780296 | tf_op jit(solution)/shard_map/ppermute | solution.py:12
where the time goes:
time: 286 us; the launch traced here: 285 us
  blocking collectives  140 us (49%)
  local copies, waits for them, and re-layouts  97 us (34%)
  starting transfers between devices  19.8 us (7%)
  matrix products  16 us (6%)
  waiting for transfers between devices  6.07 us (2%)
  other arithmetic  5.4 us (2%)
    psum x1, blocking collectives, local(): short_grad, medium_grad = lax.psum((short_grad, medium_grad), 'ctx')  140 us
    gather x3, local copies, waits for them, and re-layouts, toeplitz(): picked = jnp.take(filter_block, jnp.clip(lag_ids, 0, tap_count - 1), axis=1)  81.5 us
    ppermute x5, starting transfers between devices, passed_along(): return lax.ppermute(block, axis, route)  19.8 us
    dot_general x2, matrix products, apply_tile(): jnp.einsum('gts,sgc->tgc', matrix, field_tile, precision=highest, preferr...  11 us
    ppermute x5, waiting for transfers between devices, passed_along(): return lax.ppermute(block, axis, route)  6.07 us
  transfers between devices with their start and end apart: 5, of which 1 were waited for; matrix products, arithmetic and copies ran while one was open for 31% of the time, Pallas kernels for 0%

commit v1 on v0

v1 whole, which is shorter than its diff:
```python
import jax
import jax.numpy as jnp
from jax import lax
from jax.experimental import pallas as pl
from jax.experimental.pallas import tpu as pltpu
from jax.sharding import PartitionSpec as P

MESH = pl.DeviceIdType.MESH
f32, bf16 = jnp.float32, jnp.bfloat16
X, Z = 4, 8
N = X * Z
T = 128
L = 128
TILES = 4
GROUPS = 8
RIM = 16
KS = 7


def halves(x):
    hi = x.astype(bf16)
    lo = (x - hi.astype(f32)).astype(bf16)
    return jnp.concatenate([hi, lo], axis=-1)


def kernel(
    q_ref, k_ref, v_ref, w_ref, h_ref, og_ref, s_ref, m_ref,
    toep, halo_kv, halo_qg, rim, qext, kext, vext, wide, lhs, res,
    acc, ra, rb, gat,
    halo_send, halo_recv, rim_send, rim_recv, s1, r1, s2, r2, s3, r3,
):
    me = lax.axis_index("ctx")
    x, z = me // Z, lax.rem(me, Z)
    nxt = {"ctx": lax.rem(me + 1, N)}
    nxt2 = {"ctx": lax.rem(me + 2, N)}
    prv = {"ctx": lax.rem(me + N - 1, N)}
    prv2 = {"ctx": lax.rem(me + N - 2, N)}
    zs = [lax.rem(z + d, Z) for d in (4, 3, 5, 2, 6, 1, 7)]
    xs = [lax.rem(x + d, X) for d in (2, 1, 3)]

    barrier = pltpu.get_barrier_semaphore()
    partners = [prv, prv2, nxt] + [{"ctx": x * Z + p} for p in zs] + [{"ctx": p * Z + z} for p in xs]
    for p in partners:
        pl.semaphore_signal(barrier, 1, device_id=p, device_id_type=MESH)

    row = lax.broadcasted_iota(jnp.int32, (T, L), 0)
    col = lax.broadcasted_iota(jnp.int32, (T, L), 1)
    flip = jnp.where(lax.rem(row + col, L) == 0, 1.0, 0.0).astype(bf16)
    taps = h_ref[...].astype(f32)
    flipped = jnp.dot(h_ref[...], flip, preferred_element_type=f32)
    for g in range(TILES * GROUPS):
        for way, src in ((0, flipped), (1, taps)):
            ring = pltpu.roll(
                jnp.broadcast_to(src[g : g + 1], (T, L)), 0, 1, stride=1, stride_axis=0
            )
            near = (col <= row) if way == 0 else (row <= col)
            toep[way, g, :, :L] = jnp.where(near, ring, 0.0).astype(bf16)
            toep[way, g, :, L:] = jnp.where(near, 0.0, ring).astype(bf16)

    pl.semaphore_wait(barrier, len(partners))

    last = pl.ds(T - RIM, RIM)
    half = TILES // 2 * L
    copies = [
        (q_ref.at[last], rim.at[:, pl.ds(0, 512)], nxt),
        (k_ref.at[last, pl.ds(half, half)], rim.at[:, pl.ds(512, half)], nxt),
        (v_ref.at[last, pl.ds(half, half)], rim.at[:, pl.ds(768, half)], nxt),
        (k_ref.at[last, pl.ds(0, half)], rim.at[:, pl.ds(1024, half)], nxt2),
        (v_ref.at[last, pl.ds(0, half)], rim.at[:, pl.ds(1280, half)], nxt2),
    ]
    for a, b, p in copies:
        pltpu.make_async_remote_copy(a, b, rim_send, rim_recv, p, MESH).start()
    halos = [
        (k_ref.at[:, pl.ds(0, half)], halo_kv.at[0], nxt),
        (v_ref.at[:, pl.ds(0, half)], halo_kv.at[1], nxt),
        (q_ref.at[:, pl.ds(half, half)], halo_qg.at[0], prv),
        (og_ref.at[:, pl.ds(half, half)], halo_qg.at[1], prv),
    ]
    moving = []
    for n, (a, b, p) in enumerate(halos):
        c = pltpu.make_async_remote_copy(a, b, halo_send.at[n], halo_recv.at[n], p, MESH)
        c.start()
        moving.append(c)

    for t in range(TILES):
        lanes = slice(t * L, (t + 1) * L)
        qext[t, 8 : 8 + T] = q_ref[:, lanes].astype(f32)
        kext[t, 8 + T :] = k_ref[:, lanes].astype(f32)
        vext[t, 8 + T :] = v_ref[:, lanes].astype(f32)

    pltpu.make_async_copy(rim, rim, rim_recv).wait()
    for c in moving:
        c.wait()
    first = me == 0
    final = me == N - 1

    def unless(cond, v):
        return jnp.where(cond, 0.0, v.astype(f32))

    for t in range(TILES):
        lanes = slice(t * L, (t + 1) * L)
        qext[t, 0:8] = unless(first, rim[8:16, lanes])
        if t < TILES // 2:
            kext[t, 0:8] = unless(me <= 1, rim[8:16, 1024 + t * L : 1024 + (t + 1) * L])
            vext[t, 0:8] = unless(me <= 1, rim[8:16, 1280 + t * L : 1280 + (t + 1) * L])
            kext[t, 8 : 8 + T] = unless(first, halo_kv[0, :, lanes])
            vext[t, 8 : 8 + T] = unless(first, halo_kv[1, :, lanes])
        else:
            other = slice((t - 2) * L, (t - 1) * L)
            kext[t, T : T + 8] = unless(first, rim[8:16, 512 + (t - 2) * L : 512 + (t - 1) * L])
            vext[t, T : T + 8] = unless(first, rim[8:16, 768 + (t - 2) * L : 768 + (t - 1) * L])
            qext[t, 8 + T :] = unless(final, halo_qg[0, :, other])

    def featurize(stream, ext, t, start, rows):
        w = w_ref[stream, :, t * L : (t + 1) * L].astype(f32)
        total = w[0:1] * ext[t, pl.ds(start, rows)]
        for j in range(1, KS):
            total = total + w[j : j + 1] * ext[t, pl.ds(start - j, rows)]
        return total

    def tap_grad(kind, t, ext, parts):
        rows = []
        for j in range(KS):
            total = jnp.zeros((8, L), f32)
            for start, g in parts:
                total = total + jnp.sum((g * ext[t, pl.ds(start - j, T)]).reshape(T // 8, 8, L), axis=0)
            rows.append(jnp.sum(total, axis=0, keepdims=True))
        acc[t, kind] = jnp.concatenate(rows + [jnp.zeros((1, L), f32)], axis=0)

    own_group = col // 16

    def pick(values):
        out = values(0)
        for g in range(1, GROUPS):
            out = jnp.where(own_group == g, values(g), out)
        return out

    def conv(way, t, piece, rhs):
        filt = toep[way, t * GROUPS : (t + 1) * GROUPS]
        if piece is not None:
            filt = filt[:, :, piece * L : (piece + 1) * L]
        k = filt.shape[-1]
        res[0 : GROUPS * T] = jnp.dot(filt.reshape(GROUPS * T, k), rhs, preferred_element_type=f32)
        return pick(lambda g: res[g * T : (g + 1) * T, :L] + res[g * T : (g + 1) * T, L:])

    def lag_sums(t, square):
        for g in range(GROUPS):
            own = square(g)
            total = own[0:8]
            for i in range(1, T // 8):
                total = total + pltpu.roll(own[8 * i : 8 * i + 8], L - 8 * i, 1)
            wide[8 * g : 8 * g + 8] = total
        total = wide[pl.ds(0, 8, stride=8)]
        for r in range(1, 8):
            total = total + pltpu.roll(wide[pl.ds(r, 8, stride=8)], L - r, 1)
        acc[t, 3] = total

    nt = (((1,), (1,)), ((), ()))
    for t in range(TILES):
        lanes = slice(t * L, (t + 1) * L)
        og = og_ref[:, lanes].astype(f32)
        q_own = featurize(0, qext, t, 8, T)
        k_own = featurize(1, kext, t, 8 + T, T)
        v_own = featurize(2, vext, t, 8 + T, T)
        mixed = k_own * v_own
        grad = og * q_own
        m2, g2 = halves(mixed), halves(grad)
        mask = [jnp.where((lax.broadcasted_iota(jnp.int32, (T, 2 * L), 1) % L) // 16 == g, 1.0, 0.0).astype(bf16) for g in range(GROUPS)]
        if t < TILES // 2:
            k_prev = featurize(1, kext, t, 8, T)
            v_prev = featurize(2, vext, t, 8, T)
            mp2 = halves(k_prev * v_prev)
            both = jnp.concatenate([m2, mp2], axis=0)
            out = conv(0, t, None, both)
            tap_grad(0, t, qext, [(8, og * out)])
            back = conv(1, t, 0, g2)
            back_prev = conv(1, t, 1, g2)
            tap_grad(1, t, kext, [(8 + T, back * v_own), (8, back_prev * v_prev)])
            tap_grad(2, t, vext, [(8 + T, back * k_own), (8, back_prev * k_prev)])
            ghi, glo = g2[:, :L], g2[:, L:]
            rhs = jnp.concatenate([jnp.concatenate([ghi, ghi], 1), jnp.concatenate([glo, glo], 1)], 0)
            for g in range(GROUPS):
                lhs[g * 2 * T : g * 2 * T + T] = m2 * mask[g]
                lhs[g * 2 * T + T : (g + 1) * 2 * T] = mp2 * mask[g]
            res[...] = lax.dot_general(lhs[...], rhs, nt, preferred_element_type=f32)

            def square(g):
                a = res[g * 2 * T : g * 2 * T + T]
                b = res[g * 2 * T + T : (g + 1) * 2 * T]
                return jnp.where(row <= col, a[:, :L] + a[:, L:], b[:, :L] + b[:, L:])
        else:
            other = slice((t - 2) * L, (t - 1) * L)
            og_next = unless(final, halo_qg[1, :, other])
            q_next = featurize(0, qext, t, 8 + T, T)
            gn2 = halves(og_next * q_next)
            both = jnp.concatenate([g2, gn2], axis=0)
            out = conv(0, t, 0, m2)
            out_next = conv(0, t, 1, m2)
            tap_grad(0, t, qext, [(8, og * out), (8 + T, og_next * out_next)])
            back = conv(1, t, None, both)
            tap_grad(1, t, kext, [(8 + T, back * v_own)])
            tap_grad(2, t, vext, [(8 + T, back * k_own)])
            hi, lo = both[:, :L], both[:, L:]
            for g in range(GROUPS):
                lhs[g * T : (g + 1) * T] = m2 * mask[g]
            left = lhs[0 : GROUPS * T]
            res[0 : GROUPS * T] = lax.dot_general(
                left, jnp.concatenate([hi, hi], 1), nt, preferred_element_type=f32
            ) + lax.dot_general(left, jnp.concatenate([lo, lo], 1), nt, preferred_element_type=f32)

            def square(g):
                a = res[g * T : (g + 1) * T]
                return jnp.where(row <= col, a[:, :L], a[:, L:])
        lag_sums(t, square)

    for p in xs:
        pltpu.make_async_remote_copy(acc.at[p], ra.at[x], s1, r1, {"ctx": p * Z + z}, MESH).start()
    ra[x] = acc[x]
    three = ra.at[pl.ds(0, X - 1)]
    seven = rb.at[pl.ds(0, Z - 1)]
    pltpu.make_async_copy(three, three, r1).wait()
    total = ra[0]
    for i in range(1, X):
        total = total + ra[i]
    rb[z] = total
    for p in zs:
        pltpu.make_async_remote_copy(rb.at[z], rb.at[z], s2, r2, {"ctx": x * Z + p}, MESH).start()
    pltpu.make_async_copy(seven, seven, r2).wait()
    total = rb[0]
    for i in range(1, Z):
        total = total + rb[i]
    gat[x] = total
    for p in xs:
        pltpu.make_async_remote_copy(gat.at[x], gat.at[x], s3, r3, {"ctx": p * Z + z}, MESH).start()
    gathered = gat.at[pl.ds(0, X - 1)]
    pltpu.make_async_copy(gathered, gathered, r3).wait()
    for t in range(TILES):
        for kind in range(3):
            s_ref[kind, :, t * L : (t + 1) * L] = gat[t, kind, :KS]
        m_ref[t * GROUPS : (t + 1) * GROUPS] = gat[t, 3]
    pltpu.make_async_copy(rim, rim, rim_send).wait()
    pltpu.make_async_copy(three, three, s1).wait()
    pltpu.make_async_copy(seven, seven, s2).wait()
    pltpu.make_async_copy(gathered, gathered, s3).wait()


def local(q, k, v, w, h, og):
    V = pltpu.VMEM
    dma = pltpu.SemaphoreType.DMA
    return pl.pallas_call(
        kernel,
        out_shape=(jax.ShapeDtypeStruct((3, KS, 512), f32), jax.ShapeDtypeStruct((32, 128), f32)),
        in_specs=[pl.BlockSpec(memory_space=V)] * 6,
        out_specs=[pl.BlockSpec(memory_space=V)] * 2,
        scratch_shapes=[
            V((2, 32, T, 2 * L), bf16),
            V((2, T, 256), bf16),
            V((2, T, 256), bf16),
            V((RIM, 1536), bf16),
            V((TILES, 8 + 2 * T, L), f32),
            V((TILES, 8 + 2 * T, L), f32),
            V((TILES, 8 + 2 * T, L), f32),
            V((8 * GROUPS, L), f32),
            V((GROUPS * 2 * T, 2 * L), bf16),
            V((GROUPS * 2 * T, 2 * L), f32),
            V((TILES, 4, 8, L), f32),
            V((X, 4, 8, L), f32),
            V((Z, 4, 8, L), f32),
            V((TILES, 4, 8, L), f32),
            dma((4,)), dma((4,)), dma, dma, dma, dma, dma, dma, dma, dma,
        ],
        compiler_params=pltpu.CompilerParams(
            collective_id=0, has_side_effects=True, vmem_limit_bytes=48 << 20
        ),
        name="block",
    )(q, k, v, w, h, og)


def solution(mesh):
    return jax.shard_map(
        local,
        mesh=mesh,
        in_specs=(
            P("ctx", "dp"),
            P("ctx", "dp"),
            P("ctx", "dp"),
            P(None, None, "dp"),
            P("dp", None),
            P("ctx", "dp"),
        ),
        out_specs=(P(None, None, "dp"), P("dp", None)),
        check_vma=False,
    )
```

time: 286 us -> 41.3 us (0.14)
  blocking collectives: 140 us -> 0 us
  local copies, waits for them, and re-layouts: 97 us -> 6.27 us
  Pallas kernels: 0 us -> 34.1 us
  starting transfers between devices: 19.8 us -> 0 us
  matrix products: 16 us -> 0 us
  waiting for transfers between devices: 6.07 us -> 0 us
  other arithmetic: 5.4 us -> 0 us
    psum x1 -> x0, blocking collectives: 140 us -> none  [local(): short_grad, medium_grad = lax.psum((short_grad, medium_grad), 'ctx')]
    gather x3 -> x0, local copies, waits for them, and re-layouts: 81.5 us -> none  [toeplitz(): picked = jnp.take(filter_block, jnp.clip(lag_ids, 0, tap_count - 1), axis=1)]
    pallas_call x0 -> x1, Pallas kernels: none -> 34.1 us  [local(): pl.pallas_call(kernel, out_shape=(jax.ShapeDtypeStruct((3, KS, 512), f32)...]
    ppermute x5 -> x0, starting transfers between devices: 19.8 us -> none  [passed_along(): return lax.ppermute(block, axis, route)]
    dot_general x3 -> x0, matrix products: 16 us -> none  [the longest x2 11 us: apply_tile(): jnp.einsum('gts,sgc->tgc', matrix, field_tile, precision=highest, preferr...]
    ppermute x5 -> x0, waiting for transfers between devices: 6.07 us -> none  [passed_along(): return lax.ppermute(block, axis, route)]
    reshape x2 -> x0, local copies, waits for them, and re-layouts: 5.33 us -> none  [the longest x1 5.18 us: one_tile(): flattened = outer_prod.reshape(group_count, tile_rows * window_rows)]
    slice x7 -> x0, local copies, waits for them, and re-layouts: 4.24 us -> none  [the longest x2 1.89 us: featurize(): weights[offset]]
  transfers between devices with their start and end apart: 5 -> 0, of which waited for: 1 -> 0; matrix products, arithmetic and copies ran while one was open for 31% -> 0% of each run, Pallas kernels for 0% -> 0%
where the time goes in v1:
time: 41.3 us; the launch traced here: 41 us
  Pallas kernels  34.1 us (83%)
  local copies, waits for them, and re-layouts  6.27 us (15%)
  between operations  0.65 us (2%)
    pallas_call x1, Pallas kernels, local(): pl.pallas_call(kernel, out_shape=(jax.ShapeDtypeStruct((3, KS, 512), f32)...  34.1 us
    unnamed x14, local copies, waits for them, and re-layouts  6.27 us

profile of v1, /device:TPU:56, one launch (start us, length us, event | category | flops | bytes accessed | tf_op | source)
XLA Modules:
  0.0 41.0 jit_solution(6742658435770139596)
XLA Ops:
  0.6 0.0 copy-start
  0.6 0.9 %copy-done = bf16[128,512]{1,0:T(8,128)(2,1)S(1)} copy-done((bf16[128,512]{1,0:T(8,128)(2,1)S(1)}, bf16[128,512]{1,0:T(8,128)(2,1)}, u32[]{:S(2)}) %copy-start) | copy-done | bytes 131096
  1.5 0.0 copy-start.1
  1.5 0.9 %copy-done.1 = bf16[128,512]{1,0:T(8,128)(2,1)S(1)} copy-done((bf16[128,512]{1,0:T(8,128)(2,1)S(1)}, bf16[128,512]{1,0:T(8,128)(2,1)}, u32[]{:S(2)}) %copy-start.1) | copy-done | bytes 131096
  2.4 0.0 copy-start.2
  2.4 0.9 %copy-done.2 = bf16[128,512]{1,0:T(8,128)(2,1)S(1)} copy-done((bf16[128,512]{1,0:T(8,128)(2,1)S(1)}, bf16[128,512]{1,0:T(8,128)(2,1)}, u32[]{:S(2)}) %copy-start.2) | copy-done | bytes 131096
  3.3 0.0 copy-start.3
  3.3 0.9 %copy-done.3 = bf16[128,512]{1,0:T(8,128)(2,1)S(1)} copy-done((bf16[128,512]{1,0:T(8,128)(2,1)S(1)}, bf16[128,512]{1,0:T(8,128)(2,1)}, u32[]{:S(2)}) %copy-start.3) | copy-done | bytes 131096
  4.3 0.0 copy-start.4
  4.3 0.7 %copy-done.4 = bf16[3,7,512]{2,1,0:T(8,128)(2,1)S(1)} copy-done((bf16[3,7,512]{2,1,0:T(8,128)(2,1)S(1)}, bf16[3,7,512]{2,1,0:T(8,128)(2,1)}, u32[]{:S(2)}) %copy-start.4) | copy-done | bytes 21528
  5.0 0.0 copy-start.5
  5.0 0.7 %copy-done.5 = bf16[32,128]{1,0:T(8,128)(2,1)S(1)} copy-done((bf16[32,128]{1,0:T(8,128)(2,1)S(1)}, bf16[32,128]{1,0:T(8,128)(2,1)}, u32[]{:S(2)}) %copy-start.5) | copy-done | bytes 8216
  5.7 34.1 %block.1 = (f32[3,7,512]{2,1,0:T(8,128)S(1)}, f32[32,128]{1,0:T(8,128)S(1)}) custom-call(bf16[128,512]{1,0:T(8,128)(2,1)S(1)} %copy-done, bf16[128,512]{1,0:T(8,128)(2,1)S(1)} %copy-done.1, bf16[128,512]{1,0:T(8,128)(2,1)S(1)} %copy-done.2, bf16[3,7,512]{2,1,0:T(8,128)(2,1)S(1)} %copy-done.4, bf16[32,128]{1,0:T(8,128)(2,1)S(1)} %copy-done.5, ...), custom_call_target="tpu_custom_call" | custom-call | tf_op jit(solution)/shard_map/block/pallas_call | solution.py:250
  39.8 0.6 %copy.10 = f32[3,7,512]{2,1,0:T(8,128)} copy(f32[3,7,512]{2,1,0:T(8,128)S(1)} %get-tuple-element.4) | data formatting | bytes 86016
  40.4 0.6 %copy.11 = f32[32,128]{1,0:T(8,128)} copy(f32[32,128]{1,0:T(8,128)S(1)} %get-tuple-element.5) | data formatting | bytes 32768
Async XLA Ops:
  0.6 0.9 %copy-start = (bf16[128,512]{1,0:T(8,128)(2,1)S(1)}, bf16[128,512]{1,0:T(8,128)(2,1)}, u32[]{:S(2)}) copy-start(bf16[128,512]{1,0:T(8,128)(2,1)} %q_ref.1) | copy-start | bytes 393220
  1.5 0.9 %copy-start.1 = (bf16[128,512]{1,0:T(8,128)(2,1)S(1)}, bf16[128,512]{1,0:T(8,128)(2,1)}, u32[]{:S(2)}) copy-start(bf16[128,512]{1,0:T(8,128)(2,1)} %k_ref.1) | copy-start | bytes 393220
  2.4 0.9 %copy-start.2 = (bf16[128,512]{1,0:T(8,128)(2,1)S(1)}, bf16[128,512]{1,0:T(8,128)(2,1)}, u32[]{:S(2)}) copy-start(bf16[128,512]{1,0:T(8,128)(2,1)} %v_ref.1) | copy-start | bytes 393220
  3.3 0.9 %copy-start.3 = (bf16[128,512]{1,0:T(8,128)(2,1)S(1)}, bf16[128,512]{1,0:T(8,128)(2,1)}, u32[]{:S(2)}) copy-start(bf16[128,512]{1,0:T(8,128)(2,1)} %og_ref.1) | copy-start | bytes 393220
  4.3 0.7 %copy-start.4 = (bf16[3,7,512]{2,1,0:T(8,128)(2,1)S(1)}, bf16[3,7,512]{2,1,0:T(8,128)(2,1)}, u32[]{:S(2)}) copy-start(bf16[3,7,512]{2,1,0:T(8,128)(2,1)} %w_ref.1) | copy-start | bytes 64516
  5.0 0.7 %copy-start.5 = (bf16[32,128]{1,0:T(8,128)(2,1)S(1)}, bf16[32,128]{1,0:T(8,128)(2,1)}, u32[]{:S(2)}) copy-start(bf16[32,128]{1,0:T(8,128)(2,1)} %h_ref.1) | copy-start | bytes 24580

commit v2 on v1

v2 whole, which is shorter than its diff:
```python
import jax
import jax.numpy as jnp
from jax import lax
from jax.experimental import pallas as pl
from jax.experimental.pallas import tpu as pltpu
from jax.sharding import PartitionSpec as P

MESH = pl.DeviceIdType.MESH
f32, bf16 = jnp.float32, jnp.bfloat16
X, Z = 4, 8
N = X * Z
T = 128
L = 128
TILES = 4
GROUPS = 8
RIM = 16
KS = 7


def halves(x):
    hi = x.astype(bf16)
    lo = (x - hi.astype(f32)).astype(bf16)
    return jnp.concatenate([hi, lo], axis=-1)


def kernel(
    q_hbm, k_hbm, v_hbm, w_ref, h_ref, og_hbm, gat,
    q_ref, k_ref, v_ref, og_ref, toep, halo, rim, qext, kext, vext, wide, lhs, res,
    feats, m2s, g2s, kept, acc, ra, rb,
    loaded, halo_send, halo_recv, rim_send, rim_recv, s1, r1, s2, r2, s3, r3,
):
    me = lax.axis_index("ctx")
    x, z = me // Z, lax.rem(me, Z)
    nxt = {"ctx": lax.rem(me + 1, N)}
    nxt2 = {"ctx": lax.rem(me + 2, N)}
    prv = {"ctx": lax.rem(me + N - 1, N)}
    prv2 = {"ctx": lax.rem(me + N - 2, N)}
    zs = [lax.rem(z + d, Z) for d in (4, 3, 5, 2, 6, 1, 7)]
    xs = [lax.rem(x + d, X) for d in (2, 1, 3)]
    first = me == 0
    final = me == N - 1
    F = TILES // 2

    barrier = pltpu.get_barrier_semaphore()
    partners = [prv, prv2, nxt] + [{"ctx": x * Z + p} for p in zs] + [{"ctx": p * Z + z} for p in xs]
    for p in partners:
        pl.semaphore_signal(barrier, 1, device_id=p, device_id_type=MESH)
    loads = [
        pltpu.make_async_copy(src, dst, loaded.at[n])
        for n, (src, dst) in enumerate(
            ((q_hbm, q_ref), (k_hbm, k_ref), (v_hbm, v_ref), (og_hbm, og_ref))
        )
    ]
    for c in loads:
        c.start()
    pl.semaphore_wait(barrier, len(partners))

    last = pl.ds(T - RIM, RIM)
    half = F * L
    for a, b, p in [
        (q_hbm.at[last], rim.at[:, pl.ds(0, 512)], nxt),
        (k_hbm.at[last], rim.at[:, pl.ds(512, 512)], nxt),
        (v_hbm.at[last], rim.at[:, pl.ds(1024, 512)], nxt),
        (k_hbm.at[last, pl.ds(0, half)], rim.at[:, pl.ds(1536, half)], nxt2),
        (v_hbm.at[last, pl.ds(0, half)], rim.at[:, pl.ds(1792, half)], nxt2),
    ]:
        pltpu.make_async_remote_copy(a, b, rim_send, rim_recv, p, MESH).start()
    order = [t for pair in zip(range(F), range(F, TILES)) for t in pair]
    for t in order:
        pair, p = ((k_hbm, v_hbm), nxt) if t < F else ((q_hbm, og_hbm), prv)
        for n, src in enumerate(pair):
            pltpu.make_async_remote_copy(
                src.at[:, pl.ds(t * L, L)], halo.at[t, n], halo_send.at[t], halo_recv.at[t], p, MESH
            ).start()

    row = lax.broadcasted_iota(jnp.int32, (T, L), 0)
    col = lax.broadcasted_iota(jnp.int32, (T, L), 1)
    flip = jnp.where(lax.rem(row + col, L) == 0, 1.0, 0.0).astype(bf16)
    taps = h_ref[...].astype(f32)
    flipped = jnp.dot(h_ref[...], flip, preferred_element_type=f32)
    for g in range(TILES * GROUPS):
        for way, src in ((0, flipped), (1, taps)):
            ring = pltpu.roll(
                jnp.broadcast_to(src[g : g + 1], (T, L)), 0, 1, stride=1, stride_axis=0
            )
            near = (col <= row) if way == 0 else (row <= col)
            toep[way, 0, g] = jnp.where(near, ring, 0.0).astype(bf16)
            toep[way, 1, g] = jnp.where(near, 0.0, ring).astype(bf16)

    for c in loads:
        c.wait()
    for t in range(TILES):
        lanes = slice(t * L, (t + 1) * L)
        qext[t, 8 : 8 + T] = q_ref[:, lanes].astype(f32)
        kext[t, 8 + T :] = k_ref[:, lanes].astype(f32)
        vext[t, 8 + T :] = v_ref[:, lanes].astype(f32)

    def unless(cond, v):
        return jnp.where(cond, 0.0, v.astype(f32))

    pltpu.make_async_copy(rim, rim, rim_recv).wait()
    for t in range(TILES):
        lanes = slice(t * L, (t + 1) * L)
        qext[t, 0:8] = unless(first, rim[8:16, lanes])
        kext[t, T : T + 8] = unless(first, rim[8:16, 512 + t * L : 512 + (t + 1) * L])
        vext[t, T : T + 8] = unless(first, rim[8:16, 1024 + t * L : 1024 + (t + 1) * L])
        if t < F:
            kext[t, 0:8] = unless(me <= 1, rim[8:16, 1536 + t * L : 1536 + (t + 1) * L])
            vext[t, 0:8] = unless(me <= 1, rim[8:16, 1792 + t * L : 1792 + (t + 1) * L])

    def featurize(stream, ext, t, start, rows):
        w = w_ref[stream, :, t * L : (t + 1) * L].astype(f32)
        total = w[0:1] * ext[t, pl.ds(start, rows)]
        for j in range(1, KS):
            total = total + w[j : j + 1] * ext[t, pl.ds(start - j, rows)]
        return total

    def tap_grad(kind, t, ext, parts):
        rows = []
        for j in range(KS):
            total = jnp.zeros((8, L), f32)
            for start, g in parts:
                total = total + jnp.sum((g * ext[t, pl.ds(start - j, T)]).reshape(T // 8, 8, L), axis=0)
            rows.append(jnp.sum(total, axis=0, keepdims=True))
        return jnp.concatenate(rows + [jnp.zeros((1, L), f32)], axis=0)

    lane_group = col // 16
    wide_group = jnp.concatenate([lane_group, lane_group], axis=1)
    mask = [jnp.where(wide_group == g, 1.0, 0.0).astype(bf16) for g in range(GROUPS)]
    inside, across, both = (0,), (1,), (0, 1)
    nt = (((1,), (1,)), ((), ()))
    turn = [0]

    def result():
        turn[0] = (turn[0] + 1) % res.shape[0]
        return res.at[turn[0]]

    def conv(way, lags, t, field):
        out = result()
        filt = [toep[way, n, t * GROUPS : (t + 1) * GROUPS].reshape(GROUPS * T, T) for n in lags]
        filt = jnp.concatenate(filt, axis=1)
        out[...] = jnp.dot(filt, field, preferred_element_type=f32)
        total = out[0:T, :L] + out[0:T, L:]
        for g in range(1, GROUPS):
            total = jnp.where(lane_group == g, out[g * T : (g + 1) * T, :L] + out[g * T : (g + 1) * T, L:], total)
        return total

    def lag_sums(mix, grad, far):
        hi, lo = grad[:, :L], grad[:, L:]
        rhs = jnp.concatenate([jnp.concatenate([hi, hi], 1), jnp.concatenate([lo, lo], 1)], 0)
        for g in range(GROUPS):
            lhs[g * T : (g + 1) * T] = mix * mask[g]
        out = result()
        out[...] = lax.dot_general(lhs[...], rhs, nt, preferred_element_type=f32)
        near = row <= col
        for g in range(GROUPS):
            own = out[g * T : (g + 1) * T, :L] + out[g * T : (g + 1) * T, L:]
            own = jnp.where(near, 0.0, own) if far else jnp.where(near, own, 0.0)
            total = own[0:8]
            for i in range(1, T // 8):
                total = total + pltpu.roll(own[8 * i : 8 * i + 8], L - 8 * i, 1)
            wide[8 * g : 8 * g + 8] = total
        total = wide[pl.ds(0, 8, stride=8)]
        for r in range(1, 8):
            total = total + pltpu.roll(wide[pl.ds(r, 8, stride=8)], L - r, 1)
        return total

    for t in order:
        og = og_ref[:, t * L : (t + 1) * L].astype(f32)
        q_own = featurize(0, qext, t, 8, T)
        k_own = featurize(1, kext, t, 8 + T, T)
        v_own = featurize(2, vext, t, 8 + T, T)
        m2s[t], g2s[t] = halves(k_own * v_own), halves(og * q_own)
        if t < F:
            back = conv(1, inside, t, g2s[t])
            kept[t] = conv(1, across, t, g2s[t])
            acc[t, 1] = tap_grad(1, t, kext, [(8 + T, back * v_own)])
            acc[t, 2] = tap_grad(2, t, vext, [(8 + T, back * k_own)])
        else:
            out = conv(0, inside, t, m2s[t])
            kept[t] = conv(0, across, t, m2s[t])
            feats[t - F, 0], feats[t - F, 1] = k_own, v_own
            acc[t, 0] = tap_grad(0, t, qext, [(8, og * out)])
        acc[t, 3] = lag_sums(m2s[t], g2s[t], False)

    for t in order:
        pltpu.make_async_copy(halo.at[t], halo.at[t], halo_recv.at[t]).wait()
        if t < F:
            kext[t, 8 : 8 + T] = unless(first, halo[t, 0])
            vext[t, 8 : 8 + T] = unless(first, halo[t, 1])
            og = og_ref[:, t * L : (t + 1) * L].astype(f32)
            k_prev = featurize(1, kext, t, 8, T)
            v_prev = featurize(2, vext, t, 8, T)
            mp2 = halves(k_prev * v_prev)
            out = conv(0, both, t, jnp.concatenate([m2s[t], mp2], axis=0))
            back = kept[t]
            acc[t, 0] = tap_grad(0, t, qext, [(8, og * out)])
            acc[t, 1] += tap_grad(1, t, kext, [(8, back * v_prev)])
            acc[t, 2] += tap_grad(2, t, vext, [(8, back * k_prev)])
            acc[t, 3] += lag_sums(mp2, g2s[t], True)
        else:
            qext[t, 8 + T :] = unless(final, halo[t, 0])
            og_next = unless(final, halo[t, 1])
            gn2 = halves(og_next * featurize(0, qext, t, 8 + T, T))
            back = conv(1, both, t, jnp.concatenate([g2s[t], gn2], axis=0))
            acc[t, 0] += tap_grad(0, t, qext, [(8 + T, og_next * kept[t])])
            acc[t, 1] = tap_grad(1, t, kext, [(8 + T, back * feats[t - F, 1])])
            acc[t, 2] = tap_grad(2, t, vext, [(8 + T, back * feats[t - F, 0])])
            acc[t, 3] += lag_sums(m2s[t], gn2, True)

        @pl.when(x != t)
        def _():
            pltpu.make_async_remote_copy(acc.at[t], ra.at[x], s1, r1, {"ctx": t * Z + z}, MESH).start()

    ra[x] = acc[x]
    three = ra.at[pl.ds(0, X - 1)]
    seven = rb.at[pl.ds(0, Z - 1)]
    pltpu.make_async_copy(three, three, r1).wait()
    total = ra[0]
    for i in range(1, X):
        total = total + ra[i]
    rb[z] = total
    for p in zs:
        pltpu.make_async_remote_copy(rb.at[z], rb.at[z], s2, r2, {"ctx": x * Z + p}, MESH).start()
    pltpu.make_async_copy(seven, seven, r2).wait()
    total = rb[0]
    for i in range(1, Z):
        total = total + rb[i]
    gat[x] = total
    for p in xs:
        pltpu.make_async_remote_copy(gat.at[x], gat.at[x], s3, r3, {"ctx": p * Z + z}, MESH).start()
    gathered = gat.at[pl.ds(0, X - 1)]
    pltpu.make_async_copy(gathered, gathered, r3).wait()
    for t in order:
        pltpu.make_async_copy(halo.at[t], halo.at[t], halo_send.at[t]).wait()
    pltpu.make_async_copy(rim, rim, rim_send).wait()
    pltpu.make_async_copy(three, three, s1).wait()
    pltpu.make_async_copy(seven, seven, s2).wait()
    pltpu.make_async_copy(gathered, gathered, s3).wait()


def spread(gat, s_ref, m_ref):
    for t in range(TILES):
        for kind in range(3):
            s_ref[kind, :, t * L : (t + 1) * L] = gat[t, kind, :KS]
        m_ref[t * GROUPS : (t + 1) * GROUPS] = gat[t, 3]


def local(q, k, v, w, h, og):
    V = pltpu.VMEM
    dma = pltpu.SemaphoreType.DMA
    hbm, vmem = pl.BlockSpec(memory_space=pltpu.HBM), pl.BlockSpec(memory_space=V)
    sums = pl.pallas_call(
        kernel,
        out_shape=jax.ShapeDtypeStruct((TILES, 4, 8, L), f32),
        in_specs=[hbm, hbm, hbm, vmem, vmem, hbm],
        out_specs=vmem,
        scratch_shapes=[
            V((T, 512), bf16), V((T, 512), bf16), V((T, 512), bf16), V((T, 512), bf16),
            V((2, 2, TILES * GROUPS, T, T), bf16),
            V((TILES, 2, T, L), bf16),
            V((RIM, 2048), bf16),
            V((TILES, 8 + 2 * T, L), f32),
            V((TILES, 8 + 2 * T, L), f32),
            V((TILES, 8 + 2 * T, L), f32),
            V((8 * GROUPS, L), f32),
            V((GROUPS * T, 2 * L), bf16),
            V((4, GROUPS * T, 2 * L), f32),
            V((2, 2, T, L), f32),
            V((TILES, T, 2 * L), bf16),
            V((TILES, T, 2 * L), bf16),
            V((TILES, T, L), f32),
            V((TILES, 4, 8, L), f32),
            V((X, 4, 8, L), f32),
            V((Z, 4, 8, L), f32),
            dma((4,)), dma((TILES,)), dma((TILES,)),
            dma, dma, dma, dma, dma, dma, dma, dma,
        ],
        compiler_params=pltpu.CompilerParams(
            collective_id=0, has_side_effects=True, vmem_limit_bytes=64 << 20
        ),
        name="block",
    )(q, k, v, w, h, og)
    return pl.pallas_call(
        spread,
        out_shape=(jax.ShapeDtypeStruct((3, KS, 512), f32), jax.ShapeDtypeStruct((32, 128), f32)),
        in_specs=[vmem],
        out_specs=[vmem, vmem],
        name="spread",
    )(sums)


def solution(mesh):
    return jax.shard_map(
        local,
        mesh=mesh,
        in_specs=(
            P("ctx", "dp"),
            P("ctx", "dp"),
            P("ctx", "dp"),
            P(None, None, "dp"),
            P("dp", None),
            P("ctx", "dp"),
        ),
        out_specs=(P(None, None, "dp"), P("dp", None)),
        check_vma=False,
    )
```

time: 41.3 us -> 37.7 us (0.913)
  local copies, waits for them, and re-layouts: 6.27 us -> 0 us
  Pallas kernels: 34.1 us -> 36.9 us
    unnamed x14 -> x0, local copies, waits for them, and re-layouts: 6.27 us -> none
    pallas_call x1 -> x2, Pallas kernels: 34.1 us -> 36.9 us  [the longest x1 35.4 us: local(): pl.pallas_call(kernel, out_shape=jax.ShapeDtypeStruct((TILES, 4, 8, L), f...]
where the time goes in v2:
time: 37.7 us; the launch traced here: 37.5 us
  Pallas kernels  36.9 us (98%)
  between operations  0.64 us (2%)
    pallas_call x1, Pallas kernels, local(): pl.pallas_call(kernel, out_shape=jax.ShapeDtypeStruct((TILES, 4, 8, L), f...  35.4 us
    pallas_call x1, Pallas kernels, local(): pl.pallas_call(spread, out_shape=(jax.ShapeDtypeStruct((3, KS, 512), f32)...  1.47 us

profile of v2, /device:TPU:56, one launch (start us, length us, event | category | flops | bytes accessed | tf_op | source)
XLA Modules:
  0.0 37.5 jit_solution(9089840241344170316)
XLA Ops:
  0.6 35.4 %block.1.gat = f32[4,4,8,128]{3,2,1,0:T(8,128)} custom-call(bf16[128,512]{1,0:T(8,128)(2,1)} %q_hbm.1, bf16[128,512]{1,0:T(8,128)(2,1)} %k_hbm.1, bf16[128,512]{1,0:T(8,128)(2,1)} %v_hbm.1, bf16[3,7,512]{2,1,0:T(8,128)(2,1)} %w_ref.1, bf16[32,128]{1,0:T(8,128)(2,1)} %h_ref.1, bf16[128,512]{1,0:T(8,128)(2,1)} %og_hbm.1), custom_call_target="tpu_custom_call" | custom-call | tf_op jit(solution)/shard_map/block/pallas_call | solution.py:253
  36.0 1.5 %spread.1 = (f32[3,7,512]{2,1,0:T(8,128)}, f32[32,128]{1,0:T(8,128)}) custom-call(f32[4,4,8,128]{3,2,1,0:T(8,128)} %block.1.gat), custom_call_target="tpu_custom_call" | custom-call | tf_op jit(solution)/shard_map/spread/pallas_call | solution.py:284

commit v3 on v2

--- a/solution.py
+++ b/solution.py
@@ -24,8 +24,8 @@
 
 
 def kernel(
-    q_hbm, k_hbm, v_hbm, w_ref, h_ref, og_hbm, gat,
-    q_ref, k_ref, v_ref, og_ref, toep, halo, rim, qext, kext, vext, wide, lhs, res,
+    q_hbm, k_hbm, v_hbm, w_hbm, h_hbm, og_hbm, gat,
+    q_ref, k_ref, v_ref, w_ref, h_ref, og_ref, toep, halo, rim, qext, kext, vext, wide, lhs, res,
     feats, m2s, g2s, kept, acc, ra, rb,
     loaded, halo_send, halo_recv, rim_send, rim_recv, s1, r1, s2, r2, s3, r3,
 ):
@@ -48,7 +48,7 @@
     loads = [
         pltpu.make_async_copy(src, dst, loaded.at[n])
         for n, (src, dst) in enumerate(
-            ((q_hbm, q_ref), (k_hbm, k_ref), (v_hbm, v_ref), (og_hbm, og_ref))
+            ((h_hbm, h_ref), (q_hbm, q_ref), (k_hbm, k_ref), (v_hbm, v_ref), (og_hbm, og_ref), (w_hbm, w_ref))
         )
     ]
     for c in loads:
@@ -76,6 +76,7 @@
     row = lax.broadcasted_iota(jnp.int32, (T, L), 0)
     col = lax.broadcasted_iota(jnp.int32, (T, L), 1)
     flip = jnp.where(lax.rem(row + col, L) == 0, 1.0, 0.0).astype(bf16)
+    loads[0].wait()
     taps = h_ref[...].astype(f32)
     flipped = jnp.dot(h_ref[...], flip, preferred_element_type=f32)
     for g in range(TILES * GROUPS):
@@ -87,7 +88,7 @@
             toep[way, 0, g] = jnp.where(near, ring, 0.0).astype(bf16)
             toep[way, 1, g] = jnp.where(near, 0.0, ring).astype(bf16)
 
-    for c in loads:
+    for c in loads[1:]:
         c.wait()
     for t in range(TILES):
         lanes = slice(t * L, (t + 1) * L)
@@ -252,11 +253,11 @@
     hbm, vmem = pl.BlockSpec(memory_space=pltpu.HBM), pl.BlockSpec(memory_space=V)
     sums = pl.pallas_call(
         kernel,
-        out_shape=jax.ShapeDtypeStruct((TILES, 4, 8, L), f32),
-        in_specs=[hbm, hbm, hbm, vmem, vmem, hbm],
+        out_shape=pltpu.VMEM((TILES, 4, 8, L), f32),
+        in_specs=[hbm] * 6,
         out_specs=vmem,
         scratch_shapes=[
-            V((T, 512), bf16), V((T, 512), bf16), V((T, 512), bf16), V((T, 512), bf16),
+            V((T, 512), bf16), V((T, 512), bf16), V((T, 512), bf16), V((3, KS, 512), bf16), V((32, T), bf16), V((T, 512), bf16),
             V((2, 2, TILES * GROUPS, T, T), bf16),
             V((TILES, 2, T, L), bf16),
             V((RIM, 2048), bf16),
@@ -273,11 +274,11 @@
             V((TILES, 4, 8, L), f32),
             V((X, 4, 8, L), f32),
             V((Z, 4, 8, L), f32),
-            dma((4,)), dma((TILES,)), dma((TILES,)),
+            dma((6,)), dma((TILES,)), dma((TILES,)),
             dma, dma, dma, dma, dma, dma, dma, dma,
         ],
         compiler_params=pltpu.CompilerParams(
-            collective_id=0, has_side_effects=True, vmem_limit_bytes=64 << 20
+            collective_id=0, has_side_effects=True, vmem_limit_bytes=56 << 20
         ),
         name="block",
     )(q, k, v, w, h, og)
@@ -286,6 +287,7 @@
         out_shape=(jax.ShapeDtypeStruct((3, KS, 512), f32), jax.ShapeDtypeStruct((32, 128), f32)),
         in_specs=[vmem],
         out_specs=[vmem, vmem],
+        compiler_params=pltpu.CompilerParams(vmem_limit_bytes=1 << 20),
         name="spread",
     )(sums)
 

time: 37.7 us -> 35.5 us (0.942)
  Pallas kernels: 36.9 us -> 34.8 us
    pallas_call x1, Pallas kernels: 35.4 us -> 34.1 us  [local(): pl.pallas_call(kernel, out_shape=pltpu.VMEM((TILES, 4, 8, L), f32), in_sp...]
    pallas_call x1, Pallas kernels: 1.47 us -> 0.63 us  [local(): pl.pallas_call(spread, out_shape=(jax.ShapeDtypeStruct((3, KS, 512), f32)...]
where the time goes in v3:
time: 35.5 us; the launch traced here: 35.4 us
  Pallas kernels  34.8 us (98%)
  between operations  0.64 us (2%)
    pallas_call x1, Pallas kernels, local(): pl.pallas_call(kernel, out_shape=pltpu.VMEM((TILES, 4, 8, L), f32), in_sp...  34.1 us

profile of v3, /device:TPU:56, one launch (start us, length us, event | category | flops | bytes accessed | tf_op | source)
XLA Modules:
  0.0 35.4 jit_solution(16460961929258407947)
XLA Ops:
  0.6 34.1 %block.1.gat = f32[4,4,8,128]{3,2,1,0:T(8,128)S(1)} custom-call(bf16[128,512]{1,0:T(8,128)(2,1)} %q_hbm.1, bf16[128,512]{1,0:T(8,128)(2,1)} %k_hbm.1, bf16[128,512]{1,0:T(8,128)(2,1)} %v_hbm.1, bf16[3,7,512]{2,1,0:T(8,128)(2,1)} %w_hbm.1, bf16[32,128]{1,0:T(8,128)(2,1)} %h_hbm.1, bf16[128,512]{1,0:T(8,128)(2,1)} %og_hbm.1), custom_call_target="tpu_custom_call" | custom-call | tf_op jit(solution)/shard_map/block/pallas_call | solution.py:254
  34.8 0.6 %spread.1 = (f32[3,7,512]{2,1,0:T(8,128)}, f32[32,128]{1,0:T(8,128)}) custom-call(f32[4,4,8,128]{3,2,1,0:T(8,128)S(1)} %block.1.gat), custom_call_target="tpu_custom_call" | custom-call | tf_op jit(solution)/shard_map/spread/pallas_call | solution.py:285

commit v4 on v3

--- a/solution.py
+++ b/solution.py
@@ -98,16 +98,6 @@
 
     def unless(cond, v):
         return jnp.where(cond, 0.0, v.astype(f32))
-
-    pltpu.make_async_copy(rim, rim, rim_recv).wait()
-    for t in range(TILES):
-        lanes = slice(t * L, (t + 1) * L)
-        qext[t, 0:8] = unless(first, rim[8:16, lanes])
-        kext[t, T : T + 8] = unless(first, rim[8:16, 512 + t * L : 512 + (t + 1) * L])
-        vext[t, T : T + 8] = unless(first, rim[8:16, 1024 + t * L : 1024 + (t + 1) * L])
-        if t < F:
-            kext[t, 0:8] = unless(me <= 1, rim[8:16, 1536 + t * L : 1536 + (t + 1) * L])
-            vext[t, 0:8] = unless(me <= 1, rim[8:16, 1792 + t * L : 1792 + (t + 1) * L])
 
     def featurize(stream, ext, t, start, rows):
         w = w_ref[stream, :, t * L : (t + 1) * L].astype(f32)
@@ -166,12 +156,31 @@
             total = total + pltpu.roll(wide[pl.ds(r, 8, stride=8)], L - r, 1)
         return total
 
+    def own_fields(t, start, rows):
+        k_own = featurize(1, kext, t, 8 + T + start, rows)
+        v_own = featurize(2, vext, t, 8 + T + start, rows)
+        og = og_ref[start : start + rows, t * L : (t + 1) * L].astype(f32)
+        feats[t, 0, start : start + rows] = k_own
+        feats[t, 1, start : start + rows] = v_own
+        m2s[t, start : start + rows] = halves(k_own * v_own)
+        g2s[t, start : start + rows] = halves(og * featurize(0, qext, t, 8 + start, rows))
+
+    for t in order:
+        own_fields(t, RIM, T - RIM)
+    pltpu.make_async_copy(rim, rim, rim_recv).wait()
+    for t in range(TILES):
+        lanes = slice(t * L, (t + 1) * L)
+        qext[t, 0:8] = unless(first, rim[8:16, lanes])
+        kext[t, T : T + 8] = unless(first, rim[8:16, 512 + t * L : 512 + (t + 1) * L])
+        vext[t, T : T + 8] = unless(first, rim[8:16, 1024 + t * L : 1024 + (t + 1) * L])
+        if t < F:
+            kext[t, 0:8] = unless(me <= 1, rim[8:16, 1536 + t * L : 1536 + (t + 1) * L])
+            vext[t, 0:8] = unless(me <= 1, rim[8:16, 1792 + t * L : 1792 + (t + 1) * L])
+
     for t in order:
         og = og_ref[:, t * L : (t + 1) * L].astype(f32)
-        q_own = featurize(0, qext, t, 8, T)
-        k_own = featurize(1, kext, t, 8 + T, T)
-        v_own = featurize(2, vext, t, 8 + T, T)
-        m2s[t], g2s[t] = halves(k_own * v_own), halves(og * q_own)
+        own_fields(t, 0, RIM)
+        k_own, v_own = feats[t, 0], feats[t, 1]
         if t < F:
             back = conv(1, inside, t, g2s[t])
             kept[t] = conv(1, across, t, g2s[t])
@@ -180,7 +189,6 @@
         else:
             out = conv(0, inside, t, m2s[t])
             kept[t] = conv(0, across, t, m2s[t])
-            feats[t - F, 0], feats[t - F, 1] = k_own, v_own
             acc[t, 0] = tap_grad(0, t, qext, [(8, og * out)])
         acc[t, 3] = lag_sums(m2s[t], g2s[t], False)
 
@@ -205,8 +213,8 @@
             gn2 = halves(og_next * featurize(0, qext, t, 8 + T, T))
             back = conv(1, both, t, jnp.concatenate([g2s[t], gn2], axis=0))
             acc[t, 0] += tap_grad(0, t, qext, [(8 + T, og_next * kept[t])])
-            acc[t, 1] = tap_grad(1, t, kext, [(8 + T, back * feats[t - F, 1])])
-            acc[t, 2] = tap_grad(2, t, vext, [(8 + T, back * feats[t - F, 0])])
+            acc[t, 1] = tap_grad(1, t, kext, [(8 + T, back * feats[t, 1])])
+            acc[t, 2] = tap_grad(2, t, vext, [(8 + T, back * feats[t, 0])])
             acc[t, 3] += lag_sums(m2s[t], gn2, True)
 
         @pl.when(x != t)
@@ -267,7 +275,7 @@
             V((8 * GROUPS, L), f32),
             V((GROUPS * T, 2 * L), bf16),
             V((4, GROUPS * T, 2 * L), f32),
-            V((2, 2, T, L), f32),
+            V((TILES, 2, T, L), f32),
             V((TILES, T, 2 * L), bf16),
             V((TILES, T, 2 * L), bf16),
             V((TILES, T, L), f32),

time: 35.5 us -> 35.5 us (level)
  no operation moved by 1% of the time
where the time goes in v4:
time: 35.5 us; the launch traced here: 35.3 us
  Pallas kernels  34.7 us (98%)
  between operations  0.64 us (2%)
    pallas_call x1, Pallas kernels, local(): pl.pallas_call(kernel, out_shape=pltpu.VMEM((TILES, 4, 8, L), f32), in_sp...  34.1 us

profile of v4, /device:TPU:56, one launch (start us, length us, event | category | flops | bytes accessed | tf_op | source)
XLA Modules:
  0.0 35.3 jit_solution(4464575126593385193)
XLA Ops:
  0.6 34.1 %block.1.gat = f32[4,4,8,128]{3,2,1,0:T(8,128)S(1)} custom-call(bf16[128,512]{1,0:T(8,128)(2,1)} %q_hbm.1, bf16[128,512]{1,0:T(8,128)(2,1)} %k_hbm.1, bf16[128,512]{1,0:T(8,128)(2,1)} %v_hbm.1, bf16[3,7,512]{2,1,0:T(8,128)(2,1)} %w_hbm.1, bf16[32,128]{1,0:T(8,128)(2,1)} %h_hbm.1, bf16[128,512]{1,0:T(8,128)(2,1)} %og_hbm.1), custom_call_target="tpu_custom_call" | custom-call | tf_op jit(solution)/shard_map/block/pallas_call | solution.py:262
  34.7 0.6 %spread.1 = (f32[3,7,512]{2,1,0:T(8,128)}, f32[32,128]{1,0:T(8,128)}) custom-call(f32[4,4,8,128]{3,2,1,0:T(8,128)S(1)} %block.1.gat), custom_call_target="tpu_custom_call" | custom-call | tf_op jit(solution)/shard_map/spread/pallas_call | solution.py:293
